TPU v7x, 32 devices: a whole 2x2x4 slice. The times are simulated.
32 devices in a mesh: rep: 4 (over z), fsdp: 8 (over y, x, core).
Axes of the slice: x: 2, y: 2, z: 4, core: 2. Of those that a mesh axis runs over, the one named last changes fastest.
Arguments:
- tokens: bfloat16 [8192, 4096], P(('rep', 'fsdp')), may hold values from -6 to 6
- out_grad: bfloat16 [8192, 14336], P(('rep', 'fsdp')), may hold values from -6 to 6
- weight_blocks: bfloat16 [64, 128, 128], P('fsdp'), may hold values from -0.375 to 0.375
- block_row: int32 [64], replicated, may hold values from 0 to 31, as said below
- block_col: int32 [64], replicated, may hold values from 0 to 111
- send_list: int32 [8, 4, 3], P('fsdp'), may hold values from 0 to 8, as said below
Outputs:
- token_grad: bfloat16 [8192, 4096], P(('rep', 'fsdp'))
- grad_owned: float32 [4, 8, 3, 128, 128], P('rep', 'fsdp')
Inputs may be any that keep to these rules, and one draw needn't show every extreme that they name: The pairs (block_row[k], block_col[k]) are all distinct. For each f, every local block number 0 to 7 stands exactly once in send_list[f] over all owners and slots, in increasing order within an owner's slots, followed by the pad value 8; for each f some owner fills all 3 slots.
All inputs are finite; a program needn't handle non-finite values.
Results may differ from a plain program's by a relative error of at most 0.001.
Values may be sent and summed in bfloat16 or wider, within the bound.
A program may use at most 256 MiB of HBM per device.

v0:
```python
import jax
import jax.numpy as jnp
from jax import lax
from jax.sharding import PartitionSpec as P


def spread(products, row_ids, row_count):
    chosen = (row_ids[:, None] == jnp.arange(row_count, dtype=jnp.int32)[None, :]).astype(
        jnp.float32
    )
    return jnp.einsum("tnk,nq->tqk", products, chosen, precision=lax.Precision.HIGHEST)


def block_products(grad_cols, row_ids, col_ids, pieces, row_count):
    picked = jnp.take(grad_cols, col_ids, axis=1)
    products = jnp.einsum("tnc,nrc->tnr", picked, pieces, preferred_element_type=jnp.float32)
    return spread(products, row_ids, row_count)


def block_sums(features, grad_cols, row_ids, col_ids):
    left_cols = jnp.take(features, row_ids, axis=1)
    right_cols = jnp.take(grad_cols, col_ids, axis=1)
    return jnp.einsum("tnr,tnc->nrc", left_cols, right_cols, preferred_element_type=jnp.float32)


def local(tokens, out_grad, weight_blocks, block_row, block_col, send_list):
    rows_here = tokens.shape[0]
    block_size = weight_blocks.shape[1]
    row_count = tokens.shape[1] // block_size
    col_count = out_grad.shape[1] // block_size
    features = tokens.reshape(rows_here, row_count, block_size)
    grad_cols = out_grad.reshape(rows_here, col_count, block_size)
    all_blocks = lax.all_gather(weight_blocks, "fsdp", axis=0, tiled=True)
    spread_sum = block_products(grad_cols, block_row, block_col, all_blocks, row_count)
    token_grad = spread_sum.reshape(rows_here, row_count * block_size).astype(jnp.bfloat16)
    rep_count = lax.axis_size("rep")
    fsdp_count = lax.axis_size("fsdp")
    grad_scale = float(rows_here * rep_count * fsdp_count) ** (-0.5)
    empty_block = jnp.zeros((1, block_size, block_size), jnp.float32)
    peer_lists = send_list[0]
    shard_sums = lax.psum_scatter(
        block_sums(features, grad_cols, block_row, block_col),
        "fsdp",
        scatter_dimension=0,
        tiled=True,
    )
    padded = jnp.concatenate([shard_sums, empty_block], axis=0)
    outgoing = jnp.take(padded, peer_lists, axis=0)
    owned_blocks = jnp.sum(
        lax.all_to_all(outgoing, "rep", split_axis=0, concat_axis=0, tiled=True), axis=0
    )
    grad_owned = (owned_blocks * grad_scale)[None, None]
    return (token_grad, grad_owned)


def solution(mesh):
    return jax.shard_map(
        local,
        mesh=mesh,
        in_specs=(
            P(("rep", "fsdp"), None),
            P(("rep", "fsdp"), None),
            P("fsdp", None, None),
            P(),
            P(),
            P("fsdp", None, None),
        ),
        out_specs=(P(("rep", "fsdp"), None), P("rep", "fsdp", None, None, None)),
        check_vma=False,
    )
```

profile of v0, /device:TPU:0, one launch (start us, length us, event | category | flops | bytes accessed | tf_op | source)
XLA Modules:
  0.0 161.4 jit_solution(1455589629466250272)
XLA Ops:
  7.2 0.0 reduce-scatter.2.cloned.1.call-start
  7.2 0.7 compare_select_fusion.2
  7.9 0.7 compare_and_fusion
  8.5 0.7 compare_select_fusion.3
  9.2 0.7 compare_and_fusion.1
  9.9 10.2 %copy.21 = bf16[256,14336]{0,1:T(8,128)(2,1)} copy(bf16[256,14336]{1,0:T(8,128)(2,1)} %param.9) | data formatting | bytes 14680064 | tf_op args[1]
  20.0 10.6 %copy.22 = bf16[256,112,128]{2,0,1:T(8,128)(2,1)} copy(bf16[256,112,128]{0,2,1:T(8,128)(2,1)} %bitcast.34) | data formatting | bytes 14680064 | tf_op jit(solution)/shard_map/reshape | solution.py:32
  30.7 0.0 copy-done
  30.7 2.5 %copy.25 = bf16[256,4096]{0,1:T(8,128)(2,1)} copy(bf16[256,4096]{1,0:T(8,128)(2,1)S(1)} %copy-done) | data formatting | bytes 4194304 | tf_op args[0]
  33.1 3.2 %copy.26 = bf16[256,32,128]{2,0,1:T(8,128)(2,1)S(1)} copy(bf16[256,32,128]{0,2,1:T(8,128)(2,1)} %bitcast.35) | data formatting | bytes 4194304 | tf_op jit(solution)/shard_map/reshape | solution.py:31
  36.4 6.2 %gather_fusion.2 = bf16[64,256,128]{2,1,0:T(8,128)(2,1)} fusion(bf16[256,112,128]{2,0,1:T(8,128)(2,1)} %copy.22, s32[1024]{0:T(1024)S(1)} %pad_clamp_fusion.2), kind=kCustom, calls=%fused_computation.clone | custom fusion | bytes 8388864 | tf_op jit(solution)/shard_map/jit(_take)/gather | solution.py:15
  42.6 3.1 %gather_fusion = bf16[64,256,128]{2,1,0:T(8,128)(2,1)} fusion(bf16[256,32,128]{2,0,1:T(8,128)(2,1)S(1)} %copy.26, s32[1024]{0:T(1024)S(1)} %pad_clamp_fusion.1), kind=kCustom, calls=%fused_computation.1 | custom fusion | bytes 8388864 | tf_op jit(solution)/shard_map/jit(_take)/gather | solution.py:21
  45.7 7.0 %fusion.2 = f32[64,128,128]{2,1,0:T(8,128)} fusion(bf16[64,256,128]{2,1,0:T(8,128)(2,1)} %gather_fusion, pred[64]{0:T(512)(128)(4,1)S(1)} %compare_and_fusion.1, bf16[64,256,128]{2,1,0:T(8,128)(2,1)} %gather_fusion.2, pred[64]{0:T(512)(128)(4,1)S(1)} %compare_and_fusion), kind=kOutput, calls=%fused_computation.5 | convolution fusion | flops 541065216 | bytes 12583040 | tf_op jit(solution)/shard_map/tnr,tnc->nrc/dot_general | solution.py:23
  52.7 0.0 reduce-scatter.2.cloned.1.call-update
  52.8 0.0 all-gather.2.cloned.1.call-start
  52.8 0.7 all-gather.2.cloned.1.call-update
  53.5 0.0 copy-done.1
  53.5 0.1 copy.24
  53.6 0.1 copy.28
  53.7 0.1 reshape.86
  53.8 53.1 %reduce-scatter.2.cloned.1.call-done = f32[8,128,128]{2,1,0:T(8,128)} async-done(((f32[64,128,128]{2,1,0:T(8,128)}), f32[8,128,128]{2,1,0:T(8,128)}) %reduce-scatter.2.cloned.1.call-update) | async-done | bytes 524304 | tf_op jit(solution)/shard_map/reduce_scatter | solution.py:41
  106.9 1.1 concatenate.3
  108.0 0.6 gather_fusion.1
  108.6 1.0 broadcast_select_fusion.3
  109.6 4.6 %all-to-all-start = ((f32[4,3,128,128]{3,2,1,0:T(8,128)}), f32[4,3,128,128]{3,2,1,0:T(8,128)S(1)}, u32[]{:S(2)}, u32[]{:S(2)}) async-start(f32[4,3,128,128]{3,2,1,0:T(8,128)} %broadcast_select_fusion.3), calls=%async_computation.1 | async-start | bytes 1572864 | tf_op jit(solution)/shard_map/all_to_all | solution.py:50
  114.2 22.7 %all-gather.2.cloned.1.call-done = bf16[64,128,128]{2,1,0:T(8,128)(2,1)} async-done(((bf16[8,128,128]{2,1,0:T(8,128)(2,1)}), bf16[64,128,128]{2,1,0:T(8,128)(2,1)}) %all-gather.2.cloned.1.call-update) | async-done | bytes 2097168 | tf_op jit(solution)/shard_map/all_gather | solution.py:33
  136.9 4.2 %fusion.9 = f32[256,64,128]{2,0,1:T(8,128)S(1)} fusion(bf16[64,128,128]{2,1,0:T(8,128)(2,1)} %all-gather.2.cloned.1.call-done, bf16[64,256,128]{2,1,0:T(8,128)(2,1)} %gather_fusion.2, pred[64]{0:T(512)(128)(4,1)S(1)} %compare_and_fusion), kind=kOutput, calls=%fused_computation.13 | convolution fusion | flops 538968064 | bytes 14680128 | tf_op jit(solution)/shard_map/tnc,nrc->tnr/dot_general | solution.py:16
  141.1 0.0 copy-done.2
  141.1 10.4 %fusion.13 = bf16[32,256,128]{2,0,1:T(8,128)(2,1)S(1)} fusion(f32[256,64,128]{2,0,1:T(8,128)S(1)} %fusion.9, s32[64]{0:T(128)S(1)} %copy-done.2), kind=kOutput, calls=%fused_computation.16 | convolution fusion | flops 806356992 | bytes 10486016 | tf_op jit(solution)/shard_map/tnk,nq->tqk/dot_general | solution.py:11
  151.5 2.3 %copy.36 = bf16[32,8,32,128]{3,1,2,0:T(8,128)(2,1)} copy(bf16[32,8,32,128]{3,2,1,0:T(8,128)(2,1)S(1)} %bitcast.36) | data formatting | bytes 4194304
  153.8 0.0 all-to-all-done
  153.8 0.7 multiply_bitcast_fusion
  (9 shorter events, 0.1 us)
Async XLA Ops:
  7.2 99.8 %reduce-scatter.2.cloned.1.call-start = ((), (), s32[]{:S(2)}) async-start(), calls=%async_computation.3 | async-start | bytes 4718592 | tf_op jit(solution)/shard_map/reduce_scatter | solution.py:41
  20.0 10.7 %copy-start = (bf16[256,4096]{1,0:T(8,128)(2,1)S(1)}, bf16[256,4096]{1,0:T(8,128)(2,1)}, u32[]{:S(2)}) copy-start(bf16[256,4096]{1,0:T(8,128)(2,1)} %param.8) | copy-start | bytes 6291460
  52.7 0.8 copy-start.1
  52.8 84.1 %all-gather.2.cloned.1.call-start = ((), (), s32[]{:S(2)}) async-start(), calls=%async_computation.2 | async-start | bytes 2359296 | tf_op jit(solution)/shard_map/all_gather | solution.py:33
  109.6 44.2 %all-to-all-start = ((f32[4,3,128,128]{3,2,1,0:T(8,128)}), f32[4,3,128,128]{3,2,1,0:T(8,128)S(1)}, u32[]{:S(2)}, u32[]{:S(2)}) async-start(f32[4,3,128,128]{3,2,1,0:T(8,128)} %broadcast_select_fusion.3), calls=%async_computation.1 | async-start | bytes 1572864 | tf_op jit(solution)/shard_map/all_to_all | solution.py:50
  114.2 26.8 %copy-start.2 = (s32[64]{0:T(128)S(1)}, s32[64]{0:T(128)}, u32[]{:S(2)}) copy-start(s32[64]{0:T(128)} %param.11) | copy-start | bytes 772
Sparse Core Ops, SparseCore 0:
  52.9 53.9 reduce-scatter.1
  109.0 27.8 all-gather.1
where the time goes:
time: 162 us; the launch traced here: 161 us
  waiting for transfers between devices  76.5 us (47%)
  local copies, waits for them, and re-layouts  40.1 us (25%)
  matrix products  21.6 us (13%)
  between operations  14.1 us (9%)
  starting transfers between devices  4.69 us (3%)
  other arithmetic  4.41 us (3%)
    reduce_scatter x1, waiting for transfers between devices, local(): lax.psum_scatter(block_sums(features, grad_cols, block_row, block_col), '...  53.1 us
    all_gather x1, waiting for transfers between devices, local(): all_blocks = lax.all_gather(weight_blocks, 'fsdp', axis=0, tiled=True)  22.7 us
    unnamed x10, local copies, waits for them, and re-layouts  15 us
    reshape x1, local copies, waits for them, and re-layouts, local(): grad_cols = out_grad.reshape(rows_here, col_count, block_size)  10.6 us
    dot_general x1, matrix products, spread(): jnp.einsum('tnk,nq->tqk', products, chosen, precision=lax.Precision.HIGHEST)  10.4 us
    dot_general x1, matrix products, block_sums(): jnp.einsum('tnr,tnc->nrc', left_cols, right_cols, preferred_element_type=...  7 us
    gather x1, local copies, waits for them, and re-layouts, block_products(): picked = jnp.take(grad_cols, col_ids, axis=1)  6.24 us
    all_to_all x1, starting transfers between devices, local(): lax.all_to_all(outgoing, 'rep', split_axis=0, concat_axis=0, tiled=True)  4.61 us
  transfers between devices with their start and end apart: 3, of which 2 were waited for; matrix products, arithmetic and copies ran while one was open for 12% of the time, Pallas kernels for 0%

commit v1 on v0

v1 whole, which is shorter than its diff:
```python
import functools

import jax
import jax.numpy as jnp
from jax import lax
from jax.experimental import pallas as pl
from jax.experimental.pallas import tpu as pltpu
from jax.sharding import PartitionSpec as P

MESH = pl.DeviceIdType.MESH


def exchange(
    reps, chips, cap, scale,
    rows_ref, cols_ref, list_ref, tokens_ref, grad_ref, weight_ref,
    gathered_ref, owned_ref,
    tok, grad, pair_out, pair_in, mine, chip_in, padded, rep_out, rep_in,
    load_sem, w_send, w_recv, fw_send, fw_recv, p_send, p_recv, c_send, c_recv, r_send, r_recv,
):
    rep = lax.axis_index("rep")
    shard = lax.axis_index("fsdp")
    chip, core = shard // 2, shard % 2
    other = chip * 2 + 1 - core
    per, size = weight_ref.shape[0], weight_ref.shape[1]

    def load(source, target, sem):
        def step(b, carry):
            place = pl.ds(pl.multiple_of(b * size, size), size)
            pltpu.make_async_copy(source.at[:, place], target.at[b], sem).start()
            return carry

        lax.fori_loop(0, target.shape[0], step, 0, unroll=8)

    load(tokens_ref, tok, load_sem.at[0])
    load(grad_ref, grad, load_sem.at[1])
    own_slot = gathered_ref.at[pl.ds(shard * per, per)]
    keep = pltpu.make_async_copy(weight_ref, own_slot, load_sem.at[2])
    keep.start()

    def at(d):
        return lax.rem(chip + d, chips)

    def back(d):
        return lax.rem(chip + chips - d, chips)

    barrier = pltpu.get_barrier_semaphore()
    pl.semaphore_signal(barrier, inc=1, device_id=(rep, other), device_id_type=MESH)
    for d in range(1, chips):
        pl.semaphore_signal(
            barrier, inc=1, device_id=(rep, at(d) * 2 + core), device_id_type=MESH
        )
    for d in range(1, reps):
        pl.semaphore_signal(
            barrier, inc=1, device_id=(lax.rem(rep + d, reps), shard), device_id_type=MESH
        )
    pl.semaphore_wait(barrier, chips + reps - 1)

    sends = []

    def remote(src, dst, send, recv, device):
        copy = pltpu.make_async_remote_copy(
            src_ref=src, dst_ref=dst, send_sem=send, recv_sem=recv,
            device_id=device, device_id_type=MESH,
        )
        copy.start()
        sends.append(copy)
        return copy

    forwards = [remote(weight_ref, own_slot, fw_send.at[0], fw_recv.at[0], (rep, other))]
    arrivals = [None]
    for d in range(1, chips):
        arrivals.append(
            remote(weight_ref, own_slot, w_send.at[d], w_recv.at[d], (rep, at(d) * 2 + core))
        )

    pltpu.make_async_copy(tok, tok, load_sem.at[0]).wait()
    pltpu.make_async_copy(grad, grad, load_sem.at[1]).wait()

    def products(first, target):
        def step(j, carry):
            target[j] = lax.dot_general(
                tok[rows_ref[first + j]], grad[cols_ref[first + j]],
                (((0,), (0,)), ((), ())), preferred_element_type=jnp.float32,
            )
            return carry

        lax.fori_loop(0, per, step, 0, unroll=True)

    order = list(range(1, chips)) + [0]
    pairs, chip_copies = {}, {}

    def finish(d):
        pairs[d].wait_recv()
        mine[d] = mine[d] + pair_in[d]
        if d:
            chip_copies[d] = remote(
                mine.at[d], chip_in.at[d], c_send.at[d], c_recv.at[d],
                (rep, at(d) * 2 + core),
            )

    for n, d in enumerate(order):
        products((at(d) * 2 + 1 - core) * per, pair_out.at[d])
        pairs[d] = remote(
            pair_out.at[d], pair_in.at[d], p_send.at[d], p_recv.at[d], (rep, other)
        )
        products((at(d) * 2 + core) * per, mine.at[d])
        if n:
            finish(order[n - 1])
    finish(0)

    for d in range(1, chips):
        arrivals[d].wait_recv()
        slot = gathered_ref.at[pl.ds((back(d) * 2 + core) * per, per)]
        forwards.append(
            remote(slot, slot, fw_send.at[d], fw_recv.at[d], (rep, other))
        )

    total = mine[0]
    for d in range(1, chips):
        chip_copies[d].wait_recv()
        total = total + chip_in[d]
    padded[:per] = total * scale
    padded[per] = jnp.zeros((size, size), jnp.float32)

    rep_copies = {}
    for d in range(1, reps):
        peer = lax.rem(rep + d, reps)
        for s in range(cap):
            rep_out[d, s] = padded[list_ref[peer * cap + s]]
        rep_copies[d] = remote(
            rep_out.at[d], rep_in.at[d], r_send.at[d], r_recv.at[d], (peer, shard)
        )
    for s in range(cap):
        owned_ref[s] = padded[list_ref[rep * cap + s]]
    for d in range(1, reps):
        rep_copies[d].wait_recv()
        owned_ref[...] = owned_ref[...] + rep_in[d]
    for copy in forwards:
        copy.wait_recv()
    for copy in sends:
        copy.wait_send()
    keep.wait()


def token_kernel(count, rows_ref, cols_ref, grad_ref, weight_ref, out_ref, total):
    size = weight_ref.shape[1]
    total[...] = jnp.zeros_like(total)

    def step(k, carry):
        col = pl.multiple_of(cols_ref[k] * size, size)
        row = rows_ref[k]
        total[row] = total[row] + lax.dot_general(
            grad_ref[:, pl.ds(col, size)], weight_ref[k],
            (((1,), (1,)), ((), ())), preferred_element_type=jnp.float32,
        )
        return carry

    lax.fori_loop(0, count, step, 0, unroll=8)
    for r in range(total.shape[0]):
        out_ref[:, r * size : (r + 1) * size] = total[r].astype(out_ref.dtype)


def local(tokens, out_grad, weight_blocks, block_row, block_col, send_list):
    rows_here, width = tokens.shape
    wide = out_grad.shape[1]
    per, size = weight_blocks.shape[:2]
    reps, shards = lax.axis_size("rep"), lax.axis_size("fsdp")
    chips, cap = shards // 2, send_list.shape[2]
    count = shards * per
    scale = float(rows_here * reps * shards) ** (-0.5)
    smem = pl.BlockSpec(memory_space=pltpu.SMEM)
    vmem = pl.BlockSpec(memory_space=pltpu.VMEM)
    hbm = pl.BlockSpec(memory_space=pl.ANY)
    f32 = jnp.float32
    dma = pltpu.SemaphoreType.DMA
    gathered, owned = pl.pallas_call(
        functools.partial(exchange, reps, chips, cap, scale),
        out_shape=(
            jax.ShapeDtypeStruct((count, size, size), weight_blocks.dtype),
            jax.ShapeDtypeStruct((cap, size, size), f32),
        ),
        in_specs=[smem, smem, smem, hbm, hbm, hbm],
        out_specs=(hbm, vmem),
        scratch_shapes=[
            pltpu.VMEM((width // size, rows_here, size), tokens.dtype),
            pltpu.VMEM((wide // size, rows_here, size), out_grad.dtype),
            pltpu.VMEM((chips, per, size, size), f32),
            pltpu.VMEM((chips, per, size, size), f32),
            pltpu.VMEM((chips, per, size, size), f32),
            pltpu.VMEM((chips, per, size, size), f32),
            pltpu.VMEM((per + 1, size, size), f32),
            pltpu.VMEM((reps, cap, size, size), f32),
            pltpu.VMEM((reps, cap, size, size), f32),
            dma((3,)), dma((chips,)), dma((chips,)), dma((chips,)), dma((chips,)),
            dma((chips,)), dma((chips,)), dma((chips,)), dma((chips,)),
            dma((reps,)), dma((reps,)),
        ],
        compiler_params=pltpu.CompilerParams(
            collective_id=0, has_side_effects=True, vmem_limit_bytes=56 * 2**20
        ),
    )(block_row, block_col, send_list.reshape(-1), tokens, out_grad, weight_blocks)
    token_grad = pl.pallas_call(
        functools.partial(token_kernel, count),
        out_shape=jax.ShapeDtypeStruct((rows_here, width), jnp.bfloat16),
        in_specs=[smem, smem, vmem, vmem],
        out_specs=vmem,
        scratch_shapes=[pltpu.VMEM((width // size, rows_here, size), f32)],
        compiler_params=pltpu.CompilerParams(vmem_limit_bytes=48 * 2**20),
    )(block_row, block_col, out_grad, gathered)
    return (token_grad, owned[None, None])


def solution(mesh):
    return jax.shard_map(
        local,
        mesh=mesh,
        in_specs=(
            P(("rep", "fsdp"), None),
            P(("rep", "fsdp"), None),
            P("fsdp", None, None),
            P(),
            P(),
            P("fsdp", None, None),
        ),
        out_specs=(P(("rep", "fsdp"), None), P("rep", "fsdp", None, None, None)),
        check_vma=False,
    )
```

time: 162 us -> 71.4 us (0.44)
  waiting for transfers between devices: 76.5 us -> 0 us
  Pallas kernels: 0 us -> 66.1 us
  local copies, waits for them, and re-layouts: 40.1 us -> 3.63 us
  matrix products: 21.6 us -> 0 us
  between operations: 14.1 us -> 0.67 us
  starting transfers between devices: 4.69 us -> 0 us
  other arithmetic: 4.41 us -> 0 us
    pallas_call x0 -> x2, Pallas kernels: none -> 66.1 us  [the longest x1 58.3 us: local(): pl.pallas_call(functools.partial(exchange, reps, chips, cap, scale), out_...]
    reduce_scatter x1 -> x0, waiting for transfers between devices: 53.1 us -> none  [local(): lax.psum_scatter(block_sums(features, grad_cols, block_row, block_col), '...]
    all_gather x1 -> x0, waiting for transfers between devices: 22.7 us -> none  [local(): all_blocks = lax.all_gather(weight_blocks, 'fsdp', axis=0, tiled=True)]
    dot_general x3 -> x0, matrix products: 21.6 us -> none  [the longest x1 10.4 us: spread(): jnp.einsum('tnk,nq->tqk', products, chosen, precision=lax.Precision.HIGHEST)]
    reshape x2 -> x1, local copies, waits for them, and re-layouts: 13.9 us -> 0.6 us  [local(): send_list.reshape(-1)]
    unnamed x10, local copies, waits for them, and re-layouts: 15 us -> 3.04 us
    gather x3 -> x0, local copies, waits for them, and re-layouts: 9.95 us -> none  [the longest x1 6.24 us: block_products(): picked = jnp.take(grad_cols, col_ids, axis=1)]
    all_to_all x1 -> x0, starting transfers between devices: 4.61 us -> none  [local(): lax.all_to_all(outgoing, 'rep', split_axis=0, concat_axis=0, tiled=True)]
  transfers between devices with their start and end apart: 3 -> 0, of which waited for: 2 -> 0; matrix products, arithmetic and copies ran while one was open for 12% -> 0% of each run, Pallas kernels for 0% -> 0%
where the time goes in v1:
time: 71.4 us; the launch traced here: 70.4 us
  Pallas kernels  66.1 us (93%)
  local copies, waits for them, and re-layouts  3.63 us (5%)
    pallas_call x1, Pallas kernels, local(): pl.pallas_call(functools.partial(exchange, reps, chips, cap, scale), out_...  58.3 us
    pallas_call x1, Pallas kernels, local(): pl.pallas_call(functools.partial(token_kernel, count), out_shape=jax.Shap...  7.83 us
    unnamed x10, local copies, waits for them, and re-layouts  3.04 us

profile of v1, /device:TPU:0, one launch (start us, length us, event | category | flops | bytes accessed | tf_op | source)
XLA Modules:
  0.0 70.4 jit_solution(9985738281339347258)
XLA Ops:
  0.6 0.8 %copy.9 = s32[1,4,3]{2,1,0:T(4,128)S(1)} copy(s32[1,4,3]{1,0,2:T(1,128)} %param.11) | data formatting | bytes 96 | tf_op args[5]
  1.4 0.6 reshape.7.list_ref
  2.0 0.0 copy-start.1
  2.0 0.0 copy-start.2
  2.0 58.3 %shard_map.77 = (bf16[64,128,128]{2,1,0:T(8,128)(2,1)}, f32[3,128,128]{2,1,0:T(8,128)}) custom-call(s32[64]{0:T(128)} %rows_ref.3, s32[64]{0:T(128)} %cols_ref.3, s32[12]{0:T(128)} %reshape.7.list_ref, bf16[256,4096]{1,0:T(8,128)(2,1)} %tokens_ref.1, bf16[256,14336]{1,0:T(8,128)(2,1)} %grad_ref.3, bf16[8,128,128]{2,1,0:T(8,128)(2,1)} %weight_ref.1), custom_call_target="tpu_custom_call" | custom-call | tf_op jit(solution)/shard_map/pallas_call | solution.py:176
  60.3 0.0 copy-done.1
  60.3 0.0 copy-done.2
  60.3 0.0 copy-start
  60.3 1.6 %copy-done = bf16[64,128,128]{2,1,0:T(8,128)(2,1)S(1)} copy-done((bf16[64,128,128]{2,1,0:T(8,128)(2,1)S(1)}, bf16[64,128,128]{2,1,0:T(8,128)(2,1)}, u32[]{:S(2)}) %copy-start) | copy-done | bytes 2097176
  61.9 0.0 copy-start.3
  61.9 7.8 %shard_map.78 = bf16[256,4096]{1,0:T(8,128)(2,1)} custom-call(s32[64]{0:T(128)S(1)} %copy-done.1, s32[64]{0:T(128)S(1)} %copy-done.2, bf16[256,14336]{1,0:T(8,128)(2,1)} %grad_ref.3, bf16[64,128,128]{2,1,0:T(8,128)(2,1)S(1)} %copy-done), custom_call_target="tpu_custom_call" | custom-call | tf_op jit(solution)/shard_map/pallas_call | solution.py:202
  69.8 0.0 copy-done.3
  69.8 0.7 copy.11
Async XLA Ops:
  2.0 58.3 %copy-start.1 = (s32[64]{0:T(128)S(1)}, s32[64]{0:T(128)}, u32[]{:S(2)}) copy-start(s32[64]{0:T(128)} %rows_ref.3) | copy-start | bytes 772
  2.0 58.3 %copy-start.2 = (s32[64]{0:T(128)S(1)}, s32[64]{0:T(128)}, u32[]{:S(2)}) copy-start(s32[64]{0:T(128)} %cols_ref.3) | copy-start | bytes 772
  60.3 1.6 %copy-start = (bf16[64,128,128]{2,1,0:T(8,128)(2,1)S(1)}, bf16[64,128,128]{2,1,0:T(8,128)(2,1)}, u32[]{:S(2)}) copy-start(bf16[64,128,128]{2,1,0:T(8,128)(2,1)} %get-tuple-element.4.weight_ref) | copy-start | bytes 6291460
  61.9 7.8 %copy-start.3 = (f32[3,128,128]{2,1,0:T(8,128)S(1)}, f32[3,128,128]{2,1,0:T(8,128)}, u32[]{:S(2)}) copy-start(f32[3,128,128]{2,1,0:T(8,128)} %get-tuple-element.5) | copy-start | bytes 589828

commit v2 on v1

--- a/solution.py
+++ b/solution.py
@@ -11,12 +11,14 @@
 
 
 def exchange(
-    reps, chips, cap, scale,
-    rows_ref, cols_ref, list_ref, tokens_ref, grad_ref, weight_ref,
-    gathered_ref, owned_ref,
+    reps, chips, cap, scale, fused,
+    rows_ref, cols_ref, list_ref, chain_ref, tokens_ref, grad_ref, weight_ref,
+    result_ref, owned_ref,
     tok, grad, pair_out, pair_in, mine, chip_in, padded, rep_out, rep_in,
     load_sem, w_send, w_recv, fw_send, fw_recv, p_send, p_recv, c_send, c_recv, r_send, r_recv,
+    *inside,
 ):
+    gathered_ref = inside[0] if fused else result_ref
     rep = lax.axis_index("rep")
     shard = lax.axis_index("fsdp")
     chip, core = shard // 2, shard % 2
@@ -115,6 +117,27 @@
             remote(slot, slot, fw_send.at[d], fw_recv.at[d], (rep, other))
         )
 
+    if fused:
+        _, running, out = inside
+        count = running.shape[0] - 1
+        running[count] = jnp.zeros(running.shape[1:], jnp.float32)
+        for copy in forwards:
+            copy.wait_recv()
+        keep.wait()
+
+        def chained(k, carry):
+            running[k] = running[chain_ref[k]] + lax.dot_general(
+                grad[cols_ref[k]], gathered_ref[k],
+                (((1,), (1,)), ((), ())), preferred_element_type=jnp.float32,
+            )
+            return carry
+
+        lax.fori_loop(0, count, chained, 0, unroll=8)
+        for r in range(out.shape[1] // size):
+            out[:, r * size : (r + 1) * size] = running[chain_ref[count + r]].astype(out.dtype)
+        store = pltpu.make_async_copy(out, result_ref, load_sem.at[3])
+        store.start()
+
     total = mine[0]
     for d in range(1, chips):
         chip_copies[d].wait_recv()
@@ -126,20 +149,23 @@
     for d in range(1, reps):
         peer = lax.rem(rep + d, reps)
         for s in range(cap):
-            rep_out[d, s] = padded[list_ref[peer * cap + s]]
+            rep_out[d, s] = padded[list_ref[0, peer, s]]
         rep_copies[d] = remote(
             rep_out.at[d], rep_in.at[d], r_send.at[d], r_recv.at[d], (peer, shard)
         )
     for s in range(cap):
-        owned_ref[s] = padded[list_ref[rep * cap + s]]
+        owned_ref[s] = padded[list_ref[0, rep, s]]
     for d in range(1, reps):
         rep_copies[d].wait_recv()
         owned_ref[...] = owned_ref[...] + rep_in[d]
-    for copy in forwards:
-        copy.wait_recv()
     for copy in sends:
         copy.wait_send()
-    keep.wait()
+    if fused:
+        store.wait()
+    else:
+        for copy in forwards:
+            copy.wait_recv()
+        keep.wait()
 
 
 def token_kernel(count, rows_ref, cols_ref, grad_ref, weight_ref, out_ref, total):
@@ -173,13 +199,31 @@
     hbm = pl.BlockSpec(memory_space=pl.ANY)
     f32 = jnp.float32
     dma = pltpu.SemaphoreType.DMA
-    gathered, owned = pl.pallas_call(
-        functools.partial(exchange, reps, chips, cap, scale),
+    gathered_shape = (count, size, size)
+    inside, fused = [], count * rows_here * size * 4 <= 12 * 2**20
+    chain = block_row
+    result_shape = jax.ShapeDtypeStruct(gathered_shape, weight_blocks.dtype)
+    if fused:
+        row_total = width // size
+        result_shape = jax.ShapeDtypeStruct((rows_here, width), jnp.bfloat16)
+        inside = [
+            pltpu.VMEM(gathered_shape, weight_blocks.dtype),
+            pltpu.VMEM((count + 1, rows_here, size), f32),
+            pltpu.VMEM((rows_here, width), jnp.bfloat16),
+        ]
+        serial = jnp.arange(count, dtype=jnp.int32)
+        keys = jnp.concatenate([block_row, jnp.arange(row_total, dtype=jnp.int32)])
+        ends = jnp.minimum(jnp.arange(count + row_total, dtype=jnp.int32), count)
+        found = (keys[:, None] == block_row[None, :]) & (serial[None, :] < ends[:, None])
+        latest = jnp.max(jnp.where(found, serial[None, :], -1), axis=1)
+        chain = jnp.where(latest < 0, count, latest)
+    result, owned = pl.pallas_call(
+        functools.partial(exchange, reps, chips, cap, scale, fused),
         out_shape=(
-            jax.ShapeDtypeStruct((count, size, size), weight_blocks.dtype),
+            result_shape,
             jax.ShapeDtypeStruct((cap, size, size), f32),
         ),
-        in_specs=[smem, smem, smem, hbm, hbm, hbm],
+        in_specs=[smem, smem, smem, smem, hbm, hbm, hbm],
         out_specs=(hbm, vmem),
         scratch_shapes=[
             pltpu.VMEM((width // size, rows_here, size), tokens.dtype),
@@ -191,14 +235,17 @@
             pltpu.VMEM((per + 1, size, size), f32),
             pltpu.VMEM((reps, cap, size, size), f32),
             pltpu.VMEM((reps, cap, size, size), f32),
-            dma((3,)), dma((chips,)), dma((chips,)), dma((chips,)), dma((chips,)),
+            dma((4,)), dma((chips,)), dma((chips,)), dma((chips,)), dma((chips,)),
             dma((chips,)), dma((chips,)), dma((chips,)), dma((chips,)),
             dma((reps,)), dma((reps,)),
+            *inside,
         ],
         compiler_params=pltpu.CompilerParams(
             collective_id=0, has_side_effects=True, vmem_limit_bytes=56 * 2**20
         ),
-    )(block_row, block_col, send_list.reshape(-1), tokens, out_grad, weight_blocks)
+    )(block_row, block_col, send_list, chain, tokens, out_grad, weight_blocks)
+    if fused:
+        return (result, owned[None, None])
     token_grad = pl.pallas_call(
         functools.partial(token_kernel, count),
         out_shape=jax.ShapeDtypeStruct((rows_here, width), jnp.bfloat16),
@@ -206,7 +253,7 @@
         out_specs=vmem,
         scratch_shapes=[pltpu.VMEM((width // size, rows_here, size), f32)],
         compiler_params=pltpu.CompilerParams(vmem_limit_bytes=48 * 2**20),
-    )(block_row, block_col, out_grad, gathered)
+    )(block_row, block_col, out_grad, result)
     return (token_grad, owned[None, None])
 
 

time: 71.4 us -> 67.1 us (0.940)
  Pallas kernels: 66.1 us -> 58.2 us
  other arithmetic: 0 us -> 2 us
  local copies, waits for them, and re-layouts: 3.63 us -> 5.19 us
    pallas_call x2 -> x1, Pallas kernels: 66.1 us -> 58.2 us  [local(): pl.pallas_call(functools.partial(exchange, reps, chips, cap, scale, fused...]
    unnamed x10 -> x5, local copies, waits for them, and re-layouts: 3.04 us -> 5.19 us
    reduce_max x0 -> x1, other arithmetic: none -> 0.75 us  [local(): latest = jnp.max(jnp.where(found, serial[None, :], -1), axis=1)]
    concatenate x0 -> x1, other arithmetic: none -> 0.73 us  [local(): keys = jnp.concatenate([block_row, jnp.arange(row_total, dtype=jnp.int32)])]
where the time goes in v2:
time: 67.1 us; the launch traced here: 66.1 us
  Pallas kernels  58.2 us (87%)
  local copies, waits for them, and re-layouts  5.19 us (8%)
  other arithmetic  2 us (3%)
    pallas_call x1, Pallas kernels, local(): pl.pallas_call(functools.partial(exchange, reps, chips, cap, scale, fused...  58.2 us
    unnamed x5, local copies, waits for them, and re-layouts  5.19 us

profile of v2, /device:TPU:0, one launch (start us, length us, event | category | flops | bytes accessed | tf_op | source)
XLA Modules:
  0.0 66.1 jit_solution(15795454492356281099)
XLA Ops:
  0.6 0.7 %pad_add_fusion = (s32[96]{0:T(128)S(1)}, s32[96]{0:T(128)S(1)}) fusion(s32[32]{0:T(128)S(1)} %iota.12, s32[64]{0:T(128)} %rows_ref.1), kind=kLoop, calls=%fused_computation.4 | loop fusion | flops 192 | bytes 1152 | tf_op jit(solution)/shard_map/concatenate | solution.py:215
  1.4 0.7 %select_reduce_fusion = s32[96]{0:T(128)S(1)} fusion(s32[96]{0:T(128)S(1)} %get-tuple-element.7, s32[96]{0:T(128)S(1)} %get-tuple-element.6, s32[64]{0:T(128)} %rows_ref.1), kind=kLoop, calls=%fused_computation | loop fusion | flops 30624 | bytes 1408 | tf_op jit(solution)/shard_map/reduce_max | solution.py:218
  2.1 0.5 compare_select_fusion.chain_ref
  2.6 1.3 %copy.9.list_ref = s32[1,4,3]{2,1,0:T(4,128)} copy(s32[1,4,3]{1,0,2:T(1,128)} %param.11) | data formatting | bytes 96 | tf_op args[5]
  4.0 58.2 %shard_map.77 = (bf16[256,4096]{1,0:T(8,128)(2,1)}, f32[3,128,128]{2,1,0:T(8,128)}) custom-call(s32[64]{0:T(128)} %rows_ref.1, s32[64]{0:T(128)} %cols_ref.1, s32[1,4,3]{2,1,0:T(4,128)} %copy.9.list_ref, s32[96]{0:T(128)} %compare_select_fusion.chain_ref, bf16[256,4096]{1,0:T(8,128)(2,1)} %tokens_ref.1, bf16[256,14336]{1,0:T(8,128)(2,1)} %grad_ref.1, ...), custom_call_target="tpu_custom_call" | custom-call | tf_op jit(solution)/shard_map/pallas_call | solution.py:220
  62.2 0.0 copy-start
  62.2 3.2 %copy.12 = bf16[256,4096]{1,0:T(8,128)(2,1)} copy(bf16[256,4096]{1,0:T(8,128)(2,1)} %get-tuple-element.10) | data formatting | bytes 4194304
  65.4 0.0 copy-done
  65.4 0.7 %copy.13 = f32[1,1,3,128,128]{4,3,2,1,0:T(8,128)} copy(f32[1,1,3,128,128]{4,3,2,1,0:T(8,128)S(1)} %bitcast.1) | data formatting | bytes 393216
  (1 shorter events, 0.0 us)
Async XLA Ops:
  62.2 3.2 %copy-start = (f32[3,128,128]{2,1,0:T(8,128)S(1)}, f32[3,128,128]{2,1,0:T(8,128)}, u32[]{:S(2)}) copy-start(f32[3,128,128]{2,1,0:T(8,128)} %get-tuple-element.5) | copy-start | bytes 589828

commit v3 on v2

--- a/solution.py
+++ b/solution.py
@@ -10,12 +10,27 @@
 MESH = pl.DeviceIdType.MESH
 
 
+LEVELS = 32767.0
+
+
+def encode(values):
+    top = jnp.maximum(jnp.max(jnp.abs(values), axis=1), 1e-30)
+    codes = jnp.round(values * (LEVELS / top)[:, None, :])
+    return codes.astype(jnp.int32).astype(jnp.int16), top * (1.0 / LEVELS)
+
+
+def decode(codes, unit):
+    return codes.astype(jnp.int32).astype(jnp.float32) * unit[:, None, :]
+
+
 def exchange(
     reps, chips, cap, scale, fused,
     rows_ref, cols_ref, list_ref, chain_ref, tokens_ref, grad_ref, weight_ref,
     result_ref, owned_ref,
-    tok, grad, pair_out, pair_in, mine, chip_in, padded, rep_out, rep_in,
+    tok, grad, pair_out, pair_in, mine, chip_out, chip_in, chip_unit_out, chip_unit_in,
+    padded, codes, units, rep_out, rep_in, rep_unit_out, rep_unit_in,
     load_sem, w_send, w_recv, fw_send, fw_recv, p_send, p_recv, c_send, c_recv, r_send, r_recv,
+    cu_send, cu_recv, ru_send, ru_recv,
     *inside,
 ):
     gathered_ref = inside[0] if fused else result_ref
@@ -95,9 +110,11 @@
         pairs[d].wait_recv()
         mine[d] = mine[d] + pair_in[d]
         if d:
-            chip_copies[d] = remote(
-                mine.at[d], chip_in.at[d], c_send.at[d], c_recv.at[d],
-                (rep, at(d) * 2 + core),
+            device = (rep, at(d) * 2 + core)
+            chip_out[d], chip_unit_out[d] = encode(mine[d])
+            chip_copies[d] = (
+                remote(chip_unit_out.at[d], chip_unit_in.at[d], cu_send.at[d], cu_recv.at[d], device),
+                remote(chip_out.at[d], chip_in.at[d], c_send.at[d], c_recv.at[d], device),
             )
 
     for n, d in enumerate(order):
@@ -140,24 +157,33 @@
 
     total = mine[0]
     for d in range(1, chips):
-        chip_copies[d].wait_recv()
-        total = total + chip_in[d]
-    padded[:per] = total * scale
+        for copy in chip_copies[d]:
+            copy.wait_recv()
+        total = total + decode(chip_in[d], chip_unit_in[d])
+    total = total * scale
+    padded[:per] = total
     padded[per] = jnp.zeros((size, size), jnp.float32)
+    codes[:per], units[:per] = encode(total)
+    codes[per] = jnp.zeros((size, size), jnp.int16)
+    units[per:] = jnp.zeros((units.shape[0] - per, size), jnp.float32)
 
     rep_copies = {}
     for d in range(1, reps):
         peer = lax.rem(rep + d, reps)
         for s in range(cap):
-            rep_out[d, s] = padded[list_ref[0, peer, s]]
-        rep_copies[d] = remote(
-            rep_out.at[d], rep_in.at[d], r_send.at[d], r_recv.at[d], (peer, shard)
+            rep_out[d, s] = codes[list_ref[0, peer, s]]
+            rep_unit_out[d, s] = units[list_ref[0, peer, s]]
+        device = (peer, shard)
+        rep_copies[d] = (
+            remote(rep_unit_out.at[d], rep_unit_in.at[d], ru_send.at[d], ru_recv.at[d], device),
+            remote(rep_out.at[d], rep_in.at[d], r_send.at[d], r_recv.at[d], device),
         )
     for s in range(cap):
         owned_ref[s] = padded[list_ref[0, rep, s]]
     for d in range(1, reps):
-        rep_copies[d].wait_recv()
-        owned_ref[...] = owned_ref[...] + rep_in[d]
+        for copy in rep_copies[d]:
+            copy.wait_recv()
+        owned_ref[...] = owned_ref[...] + decode(rep_in[d], rep_unit_in[d])
     for copy in sends:
         copy.wait_send()
     if fused:
@@ -231,13 +257,21 @@
             pltpu.VMEM((chips, per, size, size), f32),
             pltpu.VMEM((chips, per, size, size), f32),
             pltpu.VMEM((chips, per, size, size), f32),
-            pltpu.VMEM((chips, per, size, size), f32),
+            pltpu.VMEM((chips, per, size, size), jnp.int16),
+            pltpu.VMEM((chips, per, size, size), jnp.int16),
+            pltpu.VMEM((chips, per, size), f32),
+            pltpu.VMEM((chips, per, size), f32),
             pltpu.VMEM((per + 1, size, size), f32),
-            pltpu.VMEM((reps, cap, size, size), f32),
-            pltpu.VMEM((reps, cap, size, size), f32),
+            pltpu.VMEM((per + 1, size, size), jnp.int16),
+            pltpu.VMEM((per + 8, size), f32),
+            pltpu.VMEM((reps, cap, size, size), jnp.int16),
+            pltpu.VMEM((reps, cap, size, size), jnp.int16),
+            pltpu.VMEM((reps, cap, size), f32),
+            pltpu.VMEM((reps, cap, size), f32),
             dma((4,)), dma((chips,)), dma((chips,)), dma((chips,)), dma((chips,)),
             dma((chips,)), dma((chips,)), dma((chips,)), dma((chips,)),
             dma((reps,)), dma((reps,)),
+            dma((chips,)), dma((chips,)), dma((reps,)), dma((reps,)),
             *inside,
         ],
         compiler_params=pltpu.CompilerParams(

time: 67.1 us -> 48.8 us (0.73); the launches traced: 66.1 us -> 48.6 us
  Pallas kernels: 58.2 us -> 40.7 us
    pallas_call x1, Pallas kernels: 58.2 us -> 40.7 us  [local(): pl.pallas_call(functools.partial(exchange, reps, chips, cap, scale, fused...]
where the time goes in v3:
time: 48.8 us; the launch traced here: 48.6 us
  Pallas kernels  40.7 us (83%)
  local copies, waits for them, and re-layouts  5.19 us (11%)
  other arithmetic  2 us (4%)
  between operations  0.66 us (1%)
    pallas_call x1, Pallas kernels, local(): pl.pallas_call(functools.partial(exchange, reps, chips, cap, scale, fused...  40.7 us
    unnamed x5, local copies, waits for them, and re-layouts  5.19 us

profile of v3, /device:TPU:0, one launch (start us, length us, event | category | flops | bytes accessed | tf_op | source)
XLA Modules:
  0.0 48.6 jit_solution(11467430593692584968)
XLA Ops:
  0.6 0.7 %pad_add_fusion = (s32[96]{0:T(128)S(1)}, s32[96]{0:T(128)S(1)}) fusion(s32[32]{0:T(128)S(1)} %iota.12, s32[64]{0:T(128)} %rows_ref.1), kind=kLoop, calls=%fused_computation.4 | loop fusion | flops 192 | bytes 1152 | tf_op jit(solution)/shard_map/concatenate | solution.py:241
  1.4 0.7 %select_reduce_fusion = s32[96]{0:T(128)S(1)} fusion(s32[96]{0:T(128)S(1)} %get-tuple-element.7, s32[96]{0:T(128)S(1)} %get-tuple-element.6, s32[64]{0:T(128)} %rows_ref.1), kind=kLoop, calls=%fused_computation | loop fusion | flops 30624 | bytes 1408 | tf_op jit(solution)/shard_map/reduce_max | solution.py:244
  2.1 0.5 %compare_select_fusion.chain_ref = s32[96]{0:T(128)} fusion(s32[96]{0:T(128)S(1)} %select_reduce_fusion), kind=kLoop, calls=%fused_computation.3 | loop fusion | flops 192 | bytes 768 | tf_op jit(solution)/shard_map/jit(_where)/select_n | solution.py:245
  2.6 1.3 %copy.9.list_ref = s32[1,4,3]{2,1,0:T(4,128)} copy(s32[1,4,3]{1,0,2:T(1,128)} %param.11) | data formatting | bytes 96 | tf_op args[5]
  4.0 40.7 %shard_map.77 = (bf16[256,4096]{1,0:T(8,128)(2,1)}, f32[3,128,128]{2,1,0:T(8,128)}) custom-call(s32[64]{0:T(128)} %rows_ref.1, s32[64]{0:T(128)} %cols_ref.1, s32[1,4,3]{2,1,0:T(4,128)} %copy.9.list_ref, s32[96]{0:T(128)} %compare_select_fusion.chain_ref, bf16[256,4096]{1,0:T(8,128)(2,1)} %tokens_ref.1, bf16[256,14336]{1,0:T(8,128)(2,1)} %grad_ref.1, ...), custom_call_target="tpu_custom_call" | custom-call | tf_op jit(solution)/shard_map/pallas_call | solution.py:246
  44.7 0.0 copy-start
  44.7 3.2 %copy.12 = bf16[256,4096]{1,0:T(8,128)(2,1)} copy(bf16[256,4096]{1,0:T(8,128)(2,1)} %get-tuple-element.10) | data formatting | bytes 4194304
  47.9 0.0 copy-done
  47.9 0.7 %copy.13 = f32[1,1,3,128,128]{4,3,2,1,0:T(8,128)} copy(f32[1,1,3,128,128]{4,3,2,1,0:T(8,128)S(1)} %bitcast.1) | data formatting | bytes 393216
  (1 shorter events, 0.0 us)
Async XLA Ops:
  44.7 3.2 %copy-start = (f32[3,128,128]{2,1,0:T(8,128)S(1)}, f32[3,128,128]{2,1,0:T(8,128)}, u32[]{:S(2)}) copy-start(f32[3,128,128]{2,1,0:T(8,128)} %get-tuple-element.5) | copy-start | bytes 589828

commit v4 on v3

--- a/solution.py
+++ b/solution.py
@@ -134,27 +134,6 @@
             remote(slot, slot, fw_send.at[d], fw_recv.at[d], (rep, other))
         )
 
-    if fused:
-        _, running, out = inside
-        count = running.shape[0] - 1
-        running[count] = jnp.zeros(running.shape[1:], jnp.float32)
-        for copy in forwards:
-            copy.wait_recv()
-        keep.wait()
-
-        def chained(k, carry):
-            running[k] = running[chain_ref[k]] + lax.dot_general(
-                grad[cols_ref[k]], gathered_ref[k],
-                (((1,), (1,)), ((), ())), preferred_element_type=jnp.float32,
-            )
-            return carry
-
-        lax.fori_loop(0, count, chained, 0, unroll=8)
-        for r in range(out.shape[1] // size):
-            out[:, r * size : (r + 1) * size] = running[chain_ref[count + r]].astype(out.dtype)
-        store = pltpu.make_async_copy(out, result_ref, load_sem.at[3])
-        store.start()
-
     total = mine[0]
     for d in range(1, chips):
         for copy in chip_copies[d]:
@@ -178,6 +157,26 @@
             remote(rep_unit_out.at[d], rep_unit_in.at[d], ru_send.at[d], ru_recv.at[d], device),
             remote(rep_out.at[d], rep_in.at[d], r_send.at[d], r_recv.at[d], device),
         )
+    if fused:
+        _, running = inside
+        out = result_ref
+        count = running.shape[0] - 1
+        running[count] = jnp.zeros(running.shape[1:], jnp.float32)
+        for copy in forwards:
+            copy.wait_recv()
+        keep.wait()
+
+        def chained(k, carry):
+            running[k] = running[chain_ref[k]] + lax.dot_general(
+                grad[cols_ref[k]], gathered_ref[k],
+                (((1,), (1,)), ((), ())), preferred_element_type=jnp.float32,
+            )
+            return carry
+
+        lax.fori_loop(0, count, chained, 0, unroll=8)
+        for r in range(out.shape[1] // size):
+            out[:, r * size : (r + 1) * size] = running[chain_ref[count + r]].astype(out.dtype)
+
     for s in range(cap):
         owned_ref[s] = padded[list_ref[0, rep, s]]
     for d in range(1, reps):
@@ -186,9 +185,7 @@
         owned_ref[...] = owned_ref[...] + decode(rep_in[d], rep_unit_in[d])
     for copy in sends:
         copy.wait_send()
-    if fused:
-        store.wait()
-    else:
+    if not fused:
         for copy in forwards:
             copy.wait_recv()
         keep.wait()
@@ -231,11 +228,10 @@
     result_shape = jax.ShapeDtypeStruct(gathered_shape, weight_blocks.dtype)
     if fused:
         row_total = width // size
-        result_shape = jax.ShapeDtypeStruct((rows_here, width), jnp.bfloat16)
+        result_shape = pltpu.VMEM((rows_here, width), jnp.bfloat16)
         inside = [
             pltpu.VMEM(gathered_shape, weight_blocks.dtype),
             pltpu.VMEM((count + 1, rows_here, size), f32),
-            pltpu.VMEM((rows_here, width), jnp.bfloat16),
         ]
         serial = jnp.arange(count, dtype=jnp.int32)
         keys = jnp.concatenate([block_row, jnp.arange(row_total, dtype=jnp.int32)])
@@ -250,7 +246,7 @@
             jax.ShapeDtypeStruct((cap, size, size), f32),
         ),
         in_specs=[smem, smem, smem, smem, hbm, hbm, hbm],
-        out_specs=(hbm, vmem),
+        out_specs=(vmem if fused else hbm, vmem),
         scratch_shapes=[
             pltpu.VMEM((width // size, rows_here, size), tokens.dtype),
             pltpu.VMEM((wide // size, rows_here, size), out_grad.dtype),
@@ -268,7 +264,7 @@
             pltpu.VMEM((reps, cap, size, size), jnp.int16),
             pltpu.VMEM((reps, cap, size), f32),
             pltpu.VMEM((reps, cap, size), f32),
-            dma((4,)), dma((chips,)), dma((chips,)), dma((chips,)), dma((chips,)),
+            dma((3,)), dma((chips,)), dma((chips,)), dma((chips,)), dma((chips,)),
             dma((chips,)), dma((chips,)), dma((chips,)), dma((chips,)),
             dma((reps,)), dma((reps,)),
             dma((chips,)), dma((chips,)), dma((reps,)), dma((reps,)),

time: 48.8 us -> 46.9 us (0.961)
  local copies, waits for them, and re-layouts: 5.19 us -> 3.34 us
    unnamed x5, local copies, waits for them, and re-layouts: 5.19 us -> 3.34 us
where the time goes in v4:
time: 46.9 us; the launch traced here: 46.7 us
  Pallas kernels  40.7 us (87%)
  local copies, waits for them, and re-layouts  3.34 us (7%)
  other arithmetic  2 us (4%)
  between operations  0.66 us (1%)
    pallas_call x1, Pallas kernels, local(): pl.pallas_call(functools.partial(exchange, reps, chips, cap, scale, fused...  40.7 us
    unnamed x5, local copies, waits for them, and re-layouts  3.34 us

profile of v4, /device:TPU:0, one launch (start us, length us, event | category | flops | bytes accessed | tf_op | source)
XLA Modules:
  0.0 46.7 jit_solution(2116987484073369422)
XLA Ops:
  0.6 0.7 %pad_add_fusion = (s32[96]{0:T(128)S(1)}, s32[96]{0:T(128)S(1)}) fusion(s32[32]{0:T(128)S(1)} %iota.12, s32[64]{0:T(128)} %rows_ref.1), kind=kLoop, calls=%fused_computation.4 | loop fusion | flops 192 | bytes 1152 | tf_op jit(solution)/shard_map/concatenate | solution.py:237
  1.4 0.7 %select_reduce_fusion = s32[96]{0:T(128)S(1)} fusion(s32[96]{0:T(128)S(1)} %get-tuple-element.7, s32[96]{0:T(128)S(1)} %get-tuple-element.6, s32[64]{0:T(128)} %rows_ref.1), kind=kLoop, calls=%fused_computation | loop fusion | flops 30624 | bytes 1408 | tf_op jit(solution)/shard_map/reduce_max | solution.py:240
  2.1 0.5 %compare_select_fusion.chain_ref = s32[96]{0:T(128)} fusion(s32[96]{0:T(128)S(1)} %select_reduce_fusion), kind=kLoop, calls=%fused_computation.3 | loop fusion | flops 192 | bytes 768 | tf_op jit(solution)/shard_map/jit(_where)/select_n | solution.py:241
  2.6 1.3 %copy.9.list_ref = s32[1,4,3]{2,1,0:T(4,128)} copy(s32[1,4,3]{1,0,2:T(1,128)} %param.11) | data formatting | bytes 96 | tf_op args[5]
  4.0 40.7 %shard_map.77 = (bf16[256,4096]{1,0:T(8,128)(2,1)S(1)}, f32[3,128,128]{2,1,0:T(8,128)}) custom-call(s32[64]{0:T(128)} %rows_ref.1, s32[64]{0:T(128)} %cols_ref.1, s32[1,4,3]{2,1,0:T(4,128)} %copy.9.list_ref, s32[96]{0:T(128)} %compare_select_fusion.chain_ref, bf16[256,4096]{1,0:T(8,128)(2,1)} %tokens_ref.1, bf16[256,14336]{1,0:T(8,128)(2,1)} %grad_ref.1, ...), custom_call_target="tpu_custom_call" | custom-call | tf_op jit(solution)/shard_map/pallas_call | solution.py:242
  44.7 0.0 copy-start
  44.7 1.3 %copy.12 = bf16[256,4096]{1,0:T(8,128)(2,1)} copy(bf16[256,4096]{1,0:T(8,128)(2,1)S(1)} %get-tuple-element.8) | data formatting | bytes 4194304
  46.0 0.0 copy-done
  46.0 0.7 %copy.13 = f32[1,1,3,128,128]{4,3,2,1,0:T(8,128)} copy(f32[1,1,3,128,128]{4,3,2,1,0:T(8,128)S(1)} %bitcast.1) | data formatting | bytes 393216
  (1 shorter events, 0.0 us)
Async XLA Ops:
  44.7 1.3 %copy-start = (f32[3,128,128]{2,1,0:T(8,128)S(1)}, f32[3,128,128]{2,1,0:T(8,128)}, u32[]{:S(2)}) copy-start(f32[3,128,128]{2,1,0:T(8,128)} %get-tuple-element.5) | copy-start | bytes 589828

commit v5 on v4

--- a/solution.py
+++ b/solution.py
@@ -150,8 +150,8 @@
     for d in range(1, reps):
         peer = lax.rem(rep + d, reps)
         for s in range(cap):
-            rep_out[d, s] = codes[list_ref[0, peer, s]]
-            rep_unit_out[d, s] = units[list_ref[0, peer, s]]
+            rep_out[d, s] = codes[list_ref[s, 0, peer]]
+            rep_unit_out[d, s] = units[list_ref[s, 0, peer]]
         device = (peer, shard)
         rep_copies[d] = (
             remote(rep_unit_out.at[d], rep_unit_in.at[d], ru_send.at[d], ru_recv.at[d], device),
@@ -178,7 +178,7 @@
             out[:, r * size : (r + 1) * size] = running[chain_ref[count + r]].astype(out.dtype)
 
     for s in range(cap):
-        owned_ref[s] = padded[list_ref[0, rep, s]]
+        owned_ref[s] = padded[list_ref[s, 0, rep]]
     for d in range(1, reps):
         for copy in rep_copies[d]:
             copy.wait_recv()
@@ -273,7 +273,7 @@
         compiler_params=pltpu.CompilerParams(
             collective_id=0, has_side_effects=True, vmem_limit_bytes=56 * 2**20
         ),
-    )(block_row, block_col, send_list, chain, tokens, out_grad, weight_blocks)
+    )(block_row, block_col, jnp.transpose(send_list, (2, 0, 1)), chain, tokens, out_grad, weight_blocks)
     if fused:
         return (result, owned[None, None])
     token_grad = pl.pallas_call(

time: 46.9 us -> 45.5 us (0.970)
  local copies, waits for them, and re-layouts: 3.34 us -> 2.01 us
    unnamed x5 -> x4, local copies, waits for them, and re-layouts: 3.34 us -> 2 us
where the time goes in v5:
time: 45.5 us; the launch traced here: 45.4 us
  Pallas kernels  40.7 us (89%)
  local copies, waits for them, and re-layouts  2.01 us (4%)
  other arithmetic  2 us (4%)
  between operations  0.65 us (1%)
    pallas_call x1, Pallas kernels, local(): pl.pallas_call(functools.partial(exchange, reps, chips, cap, scale, fused...  40.7 us
    unnamed x4, local copies, waits for them, and re-layouts  2 us

profile of v5, /device:TPU:0, one launch (start us, length us, event | category | flops | bytes accessed | tf_op | source)
XLA Modules:
  0.0 45.4 jit_solution(13064455797203377581)
XLA Ops:
  0.6 0.7 %pad_add_fusion = (s32[96]{0:T(128)S(1)}, s32[96]{0:T(128)S(1)}) fusion(s32[32]{0:T(128)S(1)} %iota.12, s32[64]{0:T(128)} %rows_ref.1), kind=kLoop, calls=%fused_computation.4 | loop fusion | flops 192 | bytes 1152 | tf_op jit(solution)/shard_map/concatenate | solution.py:237
  1.4 0.7 %select_reduce_fusion = s32[96]{0:T(128)S(1)} fusion(s32[96]{0:T(128)S(1)} %get-tuple-element.7, s32[96]{0:T(128)S(1)} %get-tuple-element.6, s32[64]{0:T(128)} %rows_ref.1), kind=kLoop, calls=%fused_computation | loop fusion | flops 30624 | bytes 1408 | tf_op jit(solution)/shard_map/reduce_max | solution.py:240
  2.1 0.5 %compare_select_fusion.chain_ref = s32[96]{0:T(128)} fusion(s32[96]{0:T(128)S(1)} %select_reduce_fusion), kind=kLoop, calls=%fused_computation.3 | loop fusion | flops 192 | bytes 768 | tf_op jit(solution)/shard_map/jit(_where)/select_n | solution.py:241
  2.6 40.7 %shard_map.77 = (bf16[256,4096]{1,0:T(8,128)(2,1)S(1)}, f32[3,128,128]{2,1,0:T(8,128)}) custom-call(s32[64]{0:T(128)} %rows_ref.1, s32[64]{0:T(128)} %cols_ref.1, s32[3,1,4]{2,1,0:T(1,128)} %bitcast.3, s32[96]{0:T(128)} %compare_select_fusion.chain_ref, bf16[256,4096]{1,0:T(8,128)(2,1)} %tokens_ref.1, bf16[256,14336]{1,0:T(8,128)(2,1)} %grad_ref.1, ...), custom_call_target="tpu_custom_call" | custom-call | tf_op jit(solution)/shard_map/pallas_call | solution.py:242
  43.3 0.0 copy-start
  43.4 1.3 %copy.10 = bf16[256,4096]{1,0:T(8,128)(2,1)} copy(bf16[256,4096]{1,0:T(8,128)(2,1)S(1)} %get-tuple-element.8) | data formatting | bytes 4194304
  44.7 0.0 copy-done
  44.7 0.7 %copy.11 = f32[1,1,3,128,128]{4,3,2,1,0:T(8,128)} copy(f32[1,1,3,128,128]{4,3,2,1,0:T(8,128)S(1)} %bitcast.2) | data formatting | bytes 393216
  (1 shorter events, 0.0 us)
Async XLA Ops:
  43.3 1.3 %copy-start = (f32[3,128,128]{2,1,0:T(8,128)S(1)}, f32[3,128,128]{2,1,0:T(8,128)}, u32[]{:S(2)}) copy-start(f32[3,128,128]{2,1,0:T(8,128)} %get-tuple-element.5) | copy-start | bytes 589828
